TPU v7x, 256 devices: a whole 4x4x8 slice. The times are simulated.
256 devices in a mesh: gx: 8 (over x, y_hi), gy: 16 (over z, core), gz: 2 (over y_lo).
Axes of the slice: x: 4, y: 4 (y_hi: 2, y_lo: 2; y = y_hi * 2 + y_lo), z: 8, core: 2. Of those that a mesh axis runs over, the one named last changes fastest.
Arguments:
- populations: float32 [27, 64, 128, 256], P(None, 'gx', 'gy', 'gz'), may hold values from 0.5 to 1.5
- soot_moments: float32 [6, 64, 128, 256], P(None, 'gx', 'gy', 'gz'), may hold values from 0.2 to 2
- growth_rate: float32 [64, 128, 256], P('gx', 'gy', 'gz'), may hold values from 0 to 0.3
- moment_rates: float32 [27], replicated, may hold values from 0.5 to 1.95
Outputs:
- next_populations: float32 [27, 64, 128, 256], P(None, 'gx', 'gy', 'gz')
- next_soot: float32 [6, 64, 128, 256], P(None, 'gx', 'gy', 'gz')
All inputs are finite; a program needn't handle non-finite values.
Results may differ from a plain program's by a relative error of at most 0.0001.
Values sent between devices are 32-bit elements; how exact they have to be, the bound alone decides.
A program may use at most 128 MiB of HBM per device.

v0:
```python
import functools

import jax
import jax.numpy as jnp
from jax import lax
from jax.experimental import pallas as pl
from jax.experimental.pallas import tpu as pltpu
from jax.sharding import PartitionSpec as P

MESH = pl.DeviceIdType.MESH
STEPS = 2
KAPPA = (0.08, 0.06, 0.05, 0.04, 0.035, 0.03)
SPEED = (0, 1, -1)
LAST = 127
SIDES = (1, 2)
CORNERS = ((1, 1), (1, 2), (2, 1), (2, 2))
SOOT = {(0, 1): 18, (0, 2): 33, (1, 1): 39, (1, 2): 45, (2, 1): 51, (2, 2): 57}
FIELDS = 63
ROWS = 168
X, XZ, XY, XYZ, Y, YZ, Z = 0, 2, 4, 8, 12, 14, 16
MESSAGES = 17


def pop(a, b, e):
    return (0, 9, 24)[a] + 3 * b + e


def block(slot):
    return 16 * slot + 8


def forward(f):
    total = f[1] + f[2]
    return (4.0 * f[0] + total, f[1] - f[2], total)


def backward(n):
    return (0.5 * (n[0] - n[2]), n[1] + n[2], n[2] - n[1])


def along(values, axis, change):
    out = {}
    for i in range(3):
        for j in range(3):
            keys = [(i, j)[:axis] + (k,) + (i, j)[axis:] for k in range(3)]
            for key, value in zip(keys, change([values[key] for key in keys])):
                out[key] = value
    return out


def moment_constants(rates_ref, consts):
    for index in range(27):
        powers = (index // 9, index // 3 % 3, index % 3)
        rate = rates_ref[index]
        consts[index] = 0.125 - 0.125 * rate
        consts[27 + index] = rate * (27.0 / 3.0 ** powers.count(2))


def collide(g, consts):
    m = g
    for axis in (2, 1, 0):
        m = along(m, axis, forward)
    scale = 1.0 / 216.0
    density = m[0, 0, 0] * scale
    u = (m[1, 0, 0] * scale, m[0, 1, 0] * scale, m[0, 0, 1] * scale)
    square = [3.0 * v * v for v in u]
    product = {(0, 1): u[0] * u[1], (0, 2): u[0] * u[2], (1, 2): u[1] * u[2]}
    n = {}
    for key, value in m.items():
        index = 9 * key[0] + 3 * key[1] + key[2]
        odd = tuple(i for i in range(3) if key[i] == 1)
        part = consts[index] * value
        if len(odd) == 3:
            n[key] = part
            continue
        if len(odd) == 0:
            balance = density
            for i in range(3):
                if key[i] == 2:
                    balance = balance + square[i]
        elif len(odd) == 1:
            balance = u[odd[0]]
        else:
            balance = product[odd]
        n[key] = part + consts[27 + index] * balance
    for axis in (0, 1, 2):
        n = along(n, axis, backward)
    return n, u


def turn(value, e):
    return value if e == 0 else pltpu.roll(value, 1 if e == 1 else LAST, 1)


def lane_of(e):
    return 0 if e == 1 else LAST


def layer_out(x, g, soot, growth, consts, F, center, faces, zs):
    lane = lax.broadcasted_iota(jnp.int32, (8, 128), 1)
    base = pl.multiple_of(16 * x + 24, 8)

    def put(field, value):
        F[field, pl.ds(base, 8), :] = value
        if faces is not None:
            side, buffer = faces
            first = 9 if side == 1 else 24
            if first <= field < first + 15:
                buffer[side - 1, field - first] = value

    n, u = collide(g, consts)
    packed = {1: None, 2: None}

    def pack(e, place, value):
        moved = pltpu.roll(value, (8 * place - lane_of(e)) % 128, 1)
        packed[e] = moved if packed[e] is None else jnp.where(lane == 8 * place, moved, packed[e])

    for a in range(3):
        for b in range(3):
            for e in range(3):
                value = turn(n[a, b, e], e)
                put(pop(a, b, e), value)
                if e:
                    pack(e, 3 * a + b, value)
    half = [0.5 * v for v in u]
    for j in range(6):
        for axis in range(3):
            plus = soot[j] * (KAPPA[j] + half[axis])
            minus = soot[j] * (KAPPA[j] - half[axis])
            if axis == 2:
                plus, minus = turn(plus, 1), turn(minus, 2)
                pack(1, 9 + j, plus)
                pack(2, 9 + j, minus)
            put(SOOT[axis, 1] + j, plus)
            put(SOOT[axis, 2] + j, minus)
        center[j, x] = soot[j] * (growth + (1.0 - 6.0 * KAPPA[j]))
    for e in SIDES:
        moved = pltpu.roll(packed[e], x, 1)
        zs[e - 1] = jnp.where(lax.rem(lane, 8) == x, moved, zs[e - 1])


def pull(F, center, x):
    g = {}
    for a in range(3):
        for b in range(3):
            for e in range(3):
                g[a, b, e] = F[pop(a, b, e), pl.ds(16 * (x - SPEED[a]) + 24 - SPEED[b], 8), :]
    soot = []
    for j in range(6):
        total = center[j, x]
        for axis in range(3):
            for side in SIDES:
                move = (16, 1, 0)[axis] * SPEED[side]
                total = total + F[SOOT[axis, side] + j, pl.ds(16 * x + 24 - move, 8), :]
        soot.append(total)
    return g, soot


def kernel(
    pops_ref, soot_ref, growth_ref, rates_ref, pops_out, soot_out,
    G, S, R, F0, F1, C0, C1, xs, xzs, xzh, xys, xyh, xyzh, ys, yh, yzs, yzh, zs, zh, consts, load_sem, send_sem, recv_sem,
):
    position = tuple(lax.axis_index(axis) for axis in ("gx", "gy", "gz"))
    counts = tuple(lax.axis_size(axis) for axis in ("gx", "gy", "gz"))

    def device(*move):
        return tuple(lax.rem(p + (m + n), n) for p, m, n in zip(position, move, counts))

    targets = [(i, j, k) for i in (0, 1, -1) for j in (0, 1, -1) for k in (0, 1) if (i, j, k) != (0, 0, 0)]
    barrier = pltpu.get_barrier_semaphore()
    for target in sorted(targets, key=lambda t: -abs(t[0])):
        pl.semaphore_signal(barrier, inc=1, device_id=device(*target), device_id_type=MESH)

    loads = [
        pltpu.make_async_copy(source, target, load_sem.at[i])
        for i, (source, target) in enumerate(
            [
                (pops_ref.at[:, 0:1], G.at[:, 0:1]),
                (pops_ref.at[:, 7:8], G.at[:, 7:8]),
                (soot_ref, S),
                (growth_ref, R),
                (pops_ref.at[:, 1:7], G.at[:, 1:7]),
            ]
        )
    ]
    for load in loads:
        load.start()
    moment_constants(rates_ref, consts)
    zs[...] = jnp.zeros_like(zs)
    xys[...] = jnp.zeros_like(xys)

    F, C = (F0, F1), (C0, C1)
    lane = lax.broadcasted_iota(jnp.int32, (8, 128), 1)
    sublane = lax.broadcasted_iota(jnp.int32, (8, 128), 0)

    def message(step, index, source, target, move):
        return pltpu.make_async_remote_copy(
            src_ref=source,
            dst_ref=target,
            send_sem=send_sem.at[step, index],
            recv_sem=recv_sem.at[step, index],
            device_id=device(*move),
            device_id_type=MESH,
        )

    def messages(step):
        out = [None] * MESSAGES
        for a in SIDES:
            first, slot = (9, 0) if a == 1 else (24, 9)
            out[X + a - 1] = message(
                step, X + a - 1, xs.at[step, a - 1], F[step].at[pl.ds(first, 15), pl.ds(block(slot), 8)], (SPEED[a], 0, 0)
            )
            out[XZ + a - 1] = message(
                step, XZ + a - 1, xzs.at[step, a - 1], xzh.at[step, a - 1], (SPEED[a], 0, 1)
            )
            out[Y + a - 1] = message(step, Y + a - 1, ys.at[step, a - 1], yh.at[step, a - 1], (0, SPEED[a], 0))
            out[YZ + a - 1] = message(step, YZ + a - 1, yzs.at[step, a - 1], yzh.at[step, a - 1], (0, SPEED[a], 1))
        for d, (a, b) in enumerate(CORNERS):
            out[XY + d] = message(step, XY + d, xys.at[step, d], xyh.at[step, d], (SPEED[a], SPEED[b], 0))
            out[XYZ + d] = message(step, XYZ + d, xys.at[step, d], xyzh.at[step, d], (SPEED[a], SPEED[b], 1))
        out[Z] = message(step, Z, zs.at[step], zh.at[step], (0, 0, 1))
        return out

    sent = [messages(step) for step in range(STEPS)]

    def pack_x(step):
        for a in SIDES:
            slot = 8 if a == 1 else 1
            packed = None
            for b in range(3):
                for e in SIDES:
                    place = 3 * (e - 1) + b
                    moved = pltpu.roll(F[step][pop(a, b, e), block(slot) : block(slot) + 8, :], (place - lane_of(e)) % 128, 1)
                    packed = moved if packed is None else jnp.where(lane == place, moved, packed)
            xzs[step, a - 1] = packed
        for d, (a, b) in enumerate(CORNERS):
            row = block(8 if a == 1 else 1) + (7 if b == 1 else 0)
            for e in range(3):
                xys[step, d, e : e + 1, :] = F[step][pop(a, b, e), row : row + 1, :]

    def pack_y(step):
        for b in SIDES:
            row = block(1) + (7 if b == 1 else 0)
            packed = None
            for a in range(3):
                for e in range(3):
                    value = F[step][pop(a, b, e), pl.ds(row, 8, stride=16), :]
                    ys[step, b - 1, 3 * a + e] = value
                    if e:
                        place = 3 * (e - 1) + a
                        moved = pltpu.roll(value, (place - lane_of(e)) % 128, 1)
                        packed = moved if packed is None else jnp.where(lane == place, moved, packed)
            yzs[step, b - 1] = packed
            for j in range(6):
                ys[step, b - 1, 9 + j] = F[step][SOOT[1, b] + j, pl.ds(row, 8, stride=16), :]

    def fix_yz(step):
        for i in (Z, Y, Y + 1, YZ, YZ + 1):
            sent[step][i].wait_recv()

        def fix_layer(x, carry):
            base = pl.multiple_of(16 * x + 24, 8)
            for e in SIDES:
                packed = pltpu.roll(zh[step, e - 1], lax.rem(128 - x, 128), 1)
                for place in range(15):
                    field = pop(place // 3, place % 3, e) if place < 9 else SOOT[2, e] + place - 9
                    moved = pltpu.roll(packed, (lane_of(e) - 8 * place) % 128, 1)
                    pltpu.store(F[step].at[field, pl.ds(base, 8), :], moved, mask=lane == lane_of(e))
            return carry

        lax.fori_loop(0, 8, fix_layer, 0)
        for b in SIDES:
            row = block(1) + (-1 if b == 1 else 8)
            packed = yzh[step, b - 1]
            for a in range(3):
                for e in range(3):
                    value = yh[step, b - 1, 3 * a + e]
                    if e:
                        place = 3 * (e - 1) + a
                        moved = pltpu.roll(packed, (lane_of(e) - place) % 128, 1)
                        value = jnp.where(lane == lane_of(e), moved, value)
                    F[step][pop(a, b, e), pl.ds(row, 8, stride=16), :] = value
            for j in range(6):
                F[step][SOOT[1, b] + j, pl.ds(row, 8, stride=16), :] = yh[step, b - 1, 9 + j]

    def fix_x(step):
        for i in list(range(X, Y)):
            sent[step][i].wait_recv()
        for a in SIDES:
            slot = 0 if a == 1 else 9
            packed = xzh[step, a - 1]
            for b in range(3):
                for e in SIDES:
                    place = 3 * (e - 1) + b
                    moved = pltpu.roll(packed, (lane_of(e) - place) % 128, 1)
                    pltpu.store(
                        F[step].at[pop(a, b, e), block(slot) : block(slot) + 8, :], moved, mask=lane == lane_of(e)
                    )
        other = ((sublane == 1) & (lane == 0)) | ((sublane == 2) & (lane == LAST))
        for d, (a, b) in enumerate(CORNERS):
            row = block(0 if a == 1 else 9) + (-1 if b == 1 else 8)
            value = jnp.where(other, xyzh[step, d], xyh[step, d])
            for e in range(3):
                F[step][pop(a, b, e), row : row + 1, :] = value[e : e + 1, :]

    def given(x):
        g = {(k // 9, k // 3 % 3, k % 3): G[k, x] for k in range(27)}
        return g, [S[j, x] for j in range(6)]

    def layer(step, x, side):
        g, soot = given(x) if step == 0 else pull(F[step - 1], C[step - 1], x)
        faces = None if side is None else (side, xs.at[step])
        layer_out(x, g, soot, R[x], consts, F[step], C[step], faces, zs.at[step])

    def result(x):
        g, soot = pull(F[STEPS - 1], C[STEPS - 1], x)
        for (a, b, e), value in g.items():
            pops_out[9 * a + 3 * b + e, x] = value
        for j in range(6):
            soot_out[j, x] = soot[j]

    def inner(body):
        def step_of(x, carry):
            body(x)
            return carry

        lax.fori_loop(1, 7, step_of, 0)

    for load in loads[:4]:
        load.wait()
    for step in range(STEPS):
        if step > 0:
            fix_yz(step - 1)
            inner(functools.partial(layer, step, side=None))
            fix_x(step - 1)
        layer(step, 0, 2)
        layer(step, 7, 1)
        pack_x(step)
        if step == 0:
            pl.semaphore_wait(barrier, len(targets))
        for i in range(X, Y):
            sent[step][i].start()
        if step == 0:
            loads[4].wait()
            inner(functools.partial(layer, step, side=None))
        pack_y(step)
        for i in (Y, Y + 1, YZ, YZ + 1, Z):
            sent[step][i].start()
    fix_yz(STEPS - 1)
    inner(result)
    fix_x(STEPS - 1)
    result(0)
    result(7)
    for step in range(STEPS):
        for copy in sent[step]:
            copy.wait_send()


def shards(populations, soot_moments, growth_rate, moment_rates):
    f32 = jnp.float32
    hbm = pl.BlockSpec(memory_space=pltpu.HBM)
    vmem = pl.BlockSpec(memory_space=pltpu.VMEM)
    return pl.pallas_call(
        kernel,
        out_shape=(pltpu.VMEM(populations.shape, f32), pltpu.VMEM(soot_moments.shape, f32)),
        in_specs=[hbm, hbm, hbm, pl.BlockSpec(memory_space=pltpu.SMEM)],
        out_specs=(vmem, vmem),
        scratch_shapes=[
            pltpu.VMEM(populations.shape, f32),
            pltpu.VMEM(soot_moments.shape, f32),
            pltpu.VMEM(growth_rate.shape, f32),
            pltpu.VMEM((FIELDS, ROWS, 128), f32),
            pltpu.VMEM((FIELDS, ROWS, 128), f32),
            pltpu.VMEM(soot_moments.shape, f32),
            pltpu.VMEM(soot_moments.shape, f32),
            pltpu.VMEM((STEPS, 2, 15, 8, 128), f32),
            pltpu.VMEM((STEPS, 2, 8, 128), f32),
            pltpu.VMEM((STEPS, 2, 8, 128), f32),
            pltpu.VMEM((STEPS, 4, 8, 128), f32),
            pltpu.VMEM((STEPS, 4, 8, 128), f32),
            pltpu.VMEM((STEPS, 4, 8, 128), f32),
            pltpu.VMEM((STEPS, 2, 15, 8, 128), f32),
            pltpu.VMEM((STEPS, 2, 15, 8, 128), f32),
            pltpu.VMEM((STEPS, 2, 8, 128), f32),
            pltpu.VMEM((STEPS, 2, 8, 128), f32),
            pltpu.VMEM((STEPS, 2, 8, 128), f32),
            pltpu.VMEM((STEPS, 2, 8, 128), f32),
            pltpu.SMEM((54,), f32),
            pltpu.SemaphoreType.DMA((5,)),
            pltpu.SemaphoreType.DMA((STEPS, MESSAGES)),
            pltpu.SemaphoreType.DMA((STEPS, MESSAGES)),
        ],
        compiler_params=pltpu.CompilerParams(
            collective_id=0, has_side_effects=True, vmem_limit_bytes=48 * 1024 * 1024
        ),
    )(populations, soot_moments, growth_rate, moment_rates)


def solution(mesh):
    in_specs = (P(None, "gx", "gy", "gz"), P(None, "gx", "gy", "gz"), P("gx", "gy", "gz"), P())
    out_specs = (P(None, "gx", "gy", "gz"), P(None, "gx", "gy", "gz"))
    return jax.shard_map(shards, mesh=mesh, in_specs=in_specs, out_specs=out_specs, check_vma=False)
```

profile of v0, /device:TPU:1, one launch (start us, length us, event | category | flops | bytes accessed | tf_op | source)
XLA Modules:
  0.0 32.3 jit_solution(15977298433057625998)
XLA Ops:
  0.6 0.0 copy-start
  0.6 1.2 %copy-done = f32[27,8,8,128]{3,2,1,0:T(8,128)S(1)} copy-done((f32[27,8,8,128]{3,2,1,0:T(8,128)S(1)}, f32[27,8,8,128]{3,2,1,0:T(8,128)}, u32[]{:S(2)}) %copy-start) | copy-done | bytes 884760
  1.8 0.0 copy-start.1
  1.8 0.9 %copy-done.1 = f32[6,8,8,128]{3,2,1,0:T(8,128)S(1)} copy-done((f32[6,8,8,128]{3,2,1,0:T(8,128)S(1)}, f32[6,8,8,128]{3,2,1,0:T(8,128)}, u32[]{:S(2)}) %copy-start.1) | copy-done | bytes 196632
  2.7 0.0 copy-start.2
  2.7 0.8 %copy-done.2 = f32[8,8,128]{2,1,0:T(8,128)S(1)} copy-done((f32[8,8,128]{2,1,0:T(8,128)S(1)}, f32[8,8,128]{2,1,0:T(8,128)}, u32[]{:S(2)}) %copy-start.2) | copy-done | bytes 32792
  3.5 0.0 copy-start.3
  3.5 0.7 %copy-done.3 = f32[27]{0:T(128)S(1)} copy-done((f32[27]{0:T(128)S(1)}, f32[27]{0:T(128)}, u32[]{:S(2)}) %copy-start.3) | copy-done | bytes 132
  4.1 26.5 %shard_map.59 = (f32[27,8,8,128]{3,2,1,0:T(8,128)S(1)}, f32[6,8,8,128]{3,2,1,0:T(8,128)S(1)}) custom-call(f32[27,8,8,128]{3,2,1,0:T(8,128)S(1)} %copy-done, f32[6,8,8,128]{3,2,1,0:T(8,128)S(1)} %copy-done.1, f32[8,8,128]{2,1,0:T(8,128)S(1)} %copy-done.2, f32[27]{0:T(128)S(1)} %copy-done.3), custom_call_target="tpu_custom_call" | custom-call | tf_op jit(solution)/shard_map/pallas_call | solution.py:363
  30.7 0.9 %copy.8 = f32[27,8,8,128]{3,2,1,0:T(8,128)} copy(f32[27,8,8,128]{3,2,1,0:T(8,128)S(1)} %get-tuple-element.2) | data formatting | bytes 1769472
  31.6 0.7 %copy.9 = f32[6,8,8,128]{3,2,1,0:T(8,128)} copy(f32[6,8,8,128]{3,2,1,0:T(8,128)S(1)} %get-tuple-element.3) | data formatting | bytes 393216
Async XLA Ops:
  0.6 1.2 %copy-start = (f32[27,8,8,128]{3,2,1,0:T(8,128)S(1)}, f32[27,8,8,128]{3,2,1,0:T(8,128)}, u32[]{:S(2)}) copy-start(f32[27,8,8,128]{3,2,1,0:T(8,128)} %pops_ref.1) | copy-start | bytes 2654212
  1.8 0.9 %copy-start.1 = (f32[6,8,8,128]{3,2,1,0:T(8,128)S(1)}, f32[6,8,8,128]{3,2,1,0:T(8,128)}, u32[]{:S(2)}) copy-start(f32[6,8,8,128]{3,2,1,0:T(8,128)} %soot_ref.1) | copy-start | bytes 589828
  2.7 0.8 %copy-start.2 = (f32[8,8,128]{2,1,0:T(8,128)S(1)}, f32[8,8,128]{2,1,0:T(8,128)}, u32[]{:S(2)}) copy-start(f32[8,8,128]{2,1,0:T(8,128)} %growth_ref.1) | copy-start | bytes 98308
  3.5 0.7 %copy-start.3 = (f32[27]{0:T(128)S(1)}, f32[27]{0:T(128)}, u32[]{:S(2)}) copy-start(f32[27]{0:T(128)} %rates_ref.1) | copy-start | bytes 328
where the time goes:
time: 32.5 us; the launch traced here: 32.3 us
  Pallas kernels  26.5 us (82%)
  local copies, waits for them, and re-layouts  5.09 us (16%)
  between operations  0.65 us (2%)
    pallas_call x1, Pallas kernels, shards(): pl.pallas_call(kernel, out_shape=(pltpu.VMEM(populations.shape, f32), plt...  26.5 us
    unnamed x10, local copies, waits for them, and re-layouts  5.09 us

commit v1 on v0

v1 whole, which is shorter than its diff:
```python
import functools

import jax
import jax.numpy as jnp
from jax import lax
from jax.experimental import pallas as pl
from jax.experimental.pallas import tpu as pltpu
from jax.sharding import PartitionSpec as P

MESH = pl.DeviceIdType.MESH
STEPS = 2
KAPPA = (0.08, 0.06, 0.05, 0.04, 0.035, 0.03)
SPEED = (0, 1, -1)
LAST = 127
SIDES = (1, 2)
CORNERS = ((1, 1), (1, 2), (2, 1), (2, 2))
SOOT = {(0, 1): 18, (0, 2): 33, (1, 1): 39, (1, 2): 45, (2, 1): 51, (2, 2): 57}
FIELDS = 63
ROWS = 168
X, XZ, XY, XYZ, Y, YZ, Z = 0, 2, 4, 8, 12, 14, 16
MESSAGES = 17


def pop(a, b, e):
    return (0, 9, 24)[a] + 3 * b + e


def block(slot):
    return 16 * slot + 8


def forward(f):
    total = f[1] + f[2]
    return (4.0 * f[0] + total, f[1] - f[2], total)


def backward(n):
    return (0.5 * (n[0] - n[2]), n[1] + n[2], n[2] - n[1])


def along(values, axis, change):
    out = {}
    for i in range(3):
        for j in range(3):
            keys = [(i, j)[:axis] + (k,) + (i, j)[axis:] for k in range(3)]
            for key, value in zip(keys, change([values[key] for key in keys])):
                out[key] = value
    return out


def moment_constants(rates_ref, consts):
    for index in range(27):
        powers = (index // 9, index // 3 % 3, index % 3)
        rate = rates_ref[index]
        consts[index] = 0.125 - 0.125 * rate
        consts[27 + index] = rate * (27.0 / 3.0 ** powers.count(2))


def collide(g, consts):
    m = g
    for axis in (2, 1, 0):
        m = along(m, axis, forward)
    scale = 1.0 / 216.0
    density = m[0, 0, 0] * scale
    u = (m[1, 0, 0] * scale, m[0, 1, 0] * scale, m[0, 0, 1] * scale)
    square = [3.0 * v * v for v in u]
    product = {(0, 1): u[0] * u[1], (0, 2): u[0] * u[2], (1, 2): u[1] * u[2]}
    n = {}
    for key, value in m.items():
        index = 9 * key[0] + 3 * key[1] + key[2]
        odd = tuple(i for i in range(3) if key[i] == 1)
        part = consts[index] * value
        if len(odd) == 3:
            n[key] = part
            continue
        if len(odd) == 0:
            balance = density
            for i in range(3):
                if key[i] == 2:
                    balance = balance + square[i]
        elif len(odd) == 1:
            balance = u[odd[0]]
        else:
            balance = product[odd]
        n[key] = part + consts[27 + index] * balance
    for axis in (0, 1, 2):
        n = along(n, axis, backward)
    return n, u


def turn(value, e):
    return value if e == 0 else pltpu.roll(value, 1 if e == 1 else LAST, 1)


def lane_of(e):
    return 0 if e == 1 else LAST


def both(lane, one, two):
    return jnp.where(lane == LAST, two, one)


def z_fields(place):
    if place < 9:
        return tuple(pop(place // 3, place % 3, e) for e in SIDES)
    return tuple(SOOT[2, e] + place - 9 for e in SIDES)


def layer_out(step, x, pops, soot_ref, growth, consts, F, center):
    rows = pl.ds(pl.multiple_of(16 * x + 24, 8), 8)
    g = {(k // 9, k // 3 % 3, k % 3): pops[k, x] for k in range(27)}
    n, u = collide(g, consts)
    for (a, b, e), value in n.items():
        F[step, pop(a, b, e), rows, :] = value
    half = [0.5 * v for v in u]
    for j in range(6):
        soot = soot_ref[j, x]
        for axis in range(3):
            F[step, SOOT[axis, 1] + j, rows, :] = soot * (KAPPA[j] + half[axis])
            F[step, SOOT[axis, 2] + j, rows, :] = soot * (KAPPA[j] - half[axis])
        center[j, x] = soot * (growth[x] + (1.0 - 6.0 * KAPPA[j]))


def turn_layer(step, x, F, zs):
    lane = lax.broadcasted_iota(jnp.int32, (8, 128), 1)
    rows = pl.ds(pl.multiple_of(16 * x + 24, 8), 8)
    past = lane - x
    packed = None
    for place in range(15):
        one, two = z_fields(place)
        plus, minus = F[step, one, rows, :], F[step, two, rows, :]
        F[step, one, rows, :] = turn(plus, 1)
        F[step, two, rows, :] = turn(minus, 2)
        moved = pltpu.roll(jnp.where(lane == 0, minus, plus), 8 * place + 1 + x, 1)
        packed = moved if place == 0 else jnp.where(past >= 8 * place, moved, packed)
    left = lax.rem(lane, 8)
    zs[step, 0] = jnp.where(left == x, packed, zs[step, 0])
    zs[step, 1] = jnp.where(left == lax.rem(x + 1, 8), packed, zs[step, 1])


def pull(step, x, F, center, pops, soot_ref):
    for a in range(3):
        for b in range(3):
            for e in range(3):
                pops[9 * a + 3 * b + e, x] = F[step, pop(a, b, e), pl.ds(16 * (x - SPEED[a]) + 24 - SPEED[b], 8), :]
    for j in range(6):
        total = center[j, x]
        for axis in range(3):
            for side in SIDES:
                move = (16, 1, 0)[axis] * SPEED[side]
                total = total + F[step, SOOT[axis, side] + j, pl.ds(16 * x + 24 - move, 8), :]
        soot_ref[j, x] = total


def kernel(
    pops_ref, soot_ref, growth_ref, rates_ref, pops, soot,
    R, F, C, xs, xzs, xzh, xys, xyh, xyzh, ys, yh, yzs, yzh, zs, zh, rates, consts, load_sem, send_sem, recv_sem,
):
    position = tuple(lax.axis_index(axis) for axis in ("gx", "gy", "gz"))
    counts = tuple(lax.axis_size(axis) for axis in ("gx", "gy", "gz"))

    def device(*move):
        return tuple(lax.rem(p + (m + n), n) for p, m, n in zip(position, move, counts))

    targets = [(i, j, k) for i in (0, 1, -1) for j in (0, 1, -1) for k in (0, 1) if (i, j, k) != (0, 0, 0)]
    barrier = pltpu.get_barrier_semaphore()
    for target in sorted(targets, key=lambda t: -abs(t[0])):
        pl.semaphore_signal(barrier, inc=1, device_id=device(*target), device_id_type=MESH)

    loads = [
        pltpu.make_async_copy(source, target, load_sem.at[i])
        for i, (source, target) in enumerate([(rates_ref, rates), (pops_ref, pops), (soot_ref, soot), (growth_ref, R)])
    ]
    for load in loads:
        load.start()
    zs[...] = jnp.zeros_like(zs)
    xys[...] = jnp.zeros_like(xys)

    lane = lax.broadcasted_iota(jnp.int32, (8, 128), 1)
    sublane = lax.broadcasted_iota(jnp.int32, (8, 128), 0)

    def message(step, index, source, target, move):
        return pltpu.make_async_remote_copy(
            src_ref=source,
            dst_ref=target,
            send_sem=send_sem.at[step, index],
            recv_sem=recv_sem.at[step, index],
            device_id=device(*move),
            device_id_type=MESH,
        )

    def messages_x(step):
        out = []
        for d, (a, b) in enumerate(CORNERS):
            out.append(message(step, XY + d, xys.at[step, d], xyh.at[step, d], (SPEED[a], SPEED[b], 0)))
        for a in SIDES:
            first, slot = (9, 0) if a == 1 else (24, 9)
            there = F.at[step, pl.ds(first, 15), pl.ds(block(slot), 8)]
            out.append(message(step, X + a - 1, xs.at[step, a - 1], there, (SPEED[a], 0, 0)))
        for d, (a, b) in enumerate(CORNERS):
            out.append(message(step, XYZ + d, xys.at[step, d], xyzh.at[step, d], (SPEED[a], SPEED[b], 1)))
        for a in SIDES:
            out.append(message(step, XZ + a - 1, xzs.at[step, a - 1], xzh.at[step, a - 1], (SPEED[a], 0, 1)))
        return out

    def messages_yz(step):
        out = []
        for b in SIDES:
            out.append(message(step, Y + b - 1, ys.at[step, b - 1], yh.at[step, b - 1], (0, SPEED[b], 0)))
        for b in SIDES:
            out.append(message(step, YZ + b - 1, yzs.at[step, b - 1], yzh.at[step, b - 1], (0, SPEED[b], 1)))
        out.append(message(step, Z, zs.at[step], zh.at[step], (0, 0, 1)))
        return out

    def packed_of(pairs):
        total = None
        for i, (one, two) in enumerate(pairs):
            value = both(lane, one, two)
            moved = pltpu.roll(value, 2 * i, 1) if i else value
            here = (lane == 2 * i) | (lane == (2 * i - 1) % 128)
            total = moved if total is None else jnp.where(here, moved, total)
        return total

    def unpacked(total, i):
        return pltpu.roll(total, 128 - 2 * i, 1) if i else total

    def pack_x(step):
        for a in SIDES:
            first, rows = (9, slice(block(8), block(8) + 8)) if a == 1 else (24, slice(block(1), block(1) + 8))
            values = [F[step, first + i, rows, :] for i in range(15)]
            for i in range(15):
                xs[step, a - 1, i] = values[i]
            xzs[step, a - 1] = packed_of([(values[3 * b + 1], values[3 * b + 2]) for b in range(3)])
        for d, (a, b) in enumerate(CORNERS):
            row = block(8 if a == 1 else 1) + (7 if b == 1 else 0)
            for e in range(3):
                xys[step, d, e : e + 1, :] = F[step, pop(a, b, e), row : row + 1, :]

    def pack_y(step):
        for b in SIDES:
            row = block(1) + (7 if b == 1 else 0)
            pairs = []
            for a in range(3):
                found = [F[step, pop(a, b, e), pl.ds(row, 8, stride=16), :] for e in range(3)]
                for e in range(3):
                    ys[step, b - 1, 3 * a + e] = found[e]
                pairs.append((found[1], found[2]))
            yzs[step, b - 1] = packed_of(pairs)
            for j in range(6):
                ys[step, b - 1, 9 + j] = F[step, SOOT[1, b] + j, pl.ds(row, 8, stride=16), :]

    def fix_yz(step):
        for copy in messages_yz(step):
            copy.wait_recv()

        plus, minus = zh[step, 0], pltpu.roll(zh[step, 1], 126, 1)

        def fix_layers(i, carry):
            for x in (2 * i, 2 * i + 1):
                rows = pl.ds(pl.multiple_of(16 * x + 24, 8), 8)
                packed = jnp.where(lax.rem(lane, 8) == x, plus, minus)
                for place in range(15):
                    moved = pltpu.roll(packed, lax.rem(128 - 8 * place - x, 128), 1)
                    for e, field in zip(SIDES, z_fields(place)):
                        pltpu.store(F.at[step, field, rows, :], moved, mask=lane == lane_of(e))
            return carry

        lax.fori_loop(0, 4, fix_layers, 0)
        for b in SIDES:
            row = block(1) + (-1 if b == 1 else 8)
            packed = yzh[step, b - 1]
            for a in range(3):
                moved = unpacked(packed, a)
                for e in range(3):
                    value = yh[step, b - 1, 3 * a + e]
                    if e:
                        value = jnp.where(lane == lane_of(e), moved, value)
                    F[step, pop(a, b, e), pl.ds(row, 8, stride=16), :] = value
            for j in range(6):
                F[step, SOOT[1, b] + j, pl.ds(row, 8, stride=16), :] = yh[step, b - 1, 9 + j]

    def fix_x(step):
        for copy in messages_x(step):
            copy.wait_recv()
        for a in SIDES:
            slot = 0 if a == 1 else 9
            packed = xzh[step, a - 1]
            for b in range(3):
                moved = unpacked(packed, b)
                for e in SIDES:
                    there = F.at[step, pop(a, b, e), block(slot) : block(slot) + 8, :]
                    pltpu.store(there, moved, mask=lane == lane_of(e))
        other = ((sublane == 1) & (lane == 0)) | ((sublane == 2) & (lane == LAST))
        for d, (a, b) in enumerate(CORNERS):
            row = block(0 if a == 1 else 9) + (-1 if b == 1 else 8)
            value = jnp.where(other, xyzh[step, d], xyh[step, d])
            for e in range(3):
                F[step, pop(a, b, e), row : row + 1, :] = value[e : e + 1, :]

    for load in loads:
        load.wait()
    moment_constants(rates, consts)

    def one_pass(step, carry):
        @pl.when(step > 0)
        def _():
            fix_yz(step - 1)
            fix_x(step - 1)

        def two_layers(i, carry):
            layers = (jnp.where(i == 0, 0, 2 * i - 1), jnp.where(i == 0, 7, 2 * i))

            @pl.when(step > 0)
            def _():
                for x in layers:
                    pull(step - 1, x, F, C, pops, soot)

            @pl.when(step < STEPS)
            def _():
                for x in layers:
                    layer_out(step, x, pops, soot, R, consts, F, C)
                for x in layers:
                    turn_layer(step, x, F, zs)

            @pl.when((step < STEPS) & (i == 0))
            def _():
                pack_x(step)

                @pl.when(step == 0)
                def _():
                    pl.semaphore_wait(barrier, len(targets))

                for copy in messages_x(step):
                    copy.start()

            return carry

        lax.fori_loop(0, 4, two_layers, 0)

        @pl.when(step < STEPS)
        def _():
            pack_y(step)
            for copy in messages_yz(step):
                copy.start()

        return carry

    lax.fori_loop(0, STEPS + 1, one_pass, 0)

    def finish(step, carry):
        for copy in messages_x(step) + messages_yz(step):
            copy.wait_send()
        return carry

    lax.fori_loop(0, STEPS, finish, 0)


def write_back(pops_ref, soot_ref, pops_out, soot_out, sem):
    copies = [
        pltpu.make_async_copy(pops_ref, pops_out, sem.at[0]),
        pltpu.make_async_copy(soot_ref, soot_out, sem.at[1]),
    ]
    for copy in copies:
        copy.start()
    for copy in copies:
        copy.wait()


def shards(populations, soot_moments, growth_rate, moment_rates):
    f32 = jnp.float32
    hbm = pl.BlockSpec(memory_space=pl.ANY)
    vmem = pl.BlockSpec(memory_space=pltpu.VMEM)
    held = pl.pallas_call(
        kernel,
        out_shape=(pltpu.VMEM(populations.shape, f32), pltpu.VMEM(soot_moments.shape, f32)),
        in_specs=[hbm, hbm, hbm, hbm],
        out_specs=(vmem, vmem),
        scratch_shapes=[
            pltpu.VMEM(growth_rate.shape, f32),
            pltpu.VMEM((STEPS, FIELDS, ROWS, 128), f32),
            pltpu.VMEM(soot_moments.shape, f32),
            pltpu.VMEM((STEPS, 2, 15, 8, 128), f32),
            pltpu.VMEM((STEPS, 2, 8, 128), f32),
            pltpu.VMEM((STEPS, 2, 8, 128), f32),
            pltpu.VMEM((STEPS, 4, 8, 128), f32),
            pltpu.VMEM((STEPS, 4, 8, 128), f32),
            pltpu.VMEM((STEPS, 4, 8, 128), f32),
            pltpu.VMEM((STEPS, 2, 15, 8, 128), f32),
            pltpu.VMEM((STEPS, 2, 15, 8, 128), f32),
            pltpu.VMEM((STEPS, 2, 8, 128), f32),
            pltpu.VMEM((STEPS, 2, 8, 128), f32),
            pltpu.VMEM((STEPS, 2, 8, 128), f32),
            pltpu.VMEM((STEPS, 2, 8, 128), f32),
            pltpu.SMEM((27,), f32),
            pltpu.SMEM((54,), f32),
            pltpu.SemaphoreType.DMA((4,)),
            pltpu.SemaphoreType.DMA((STEPS, MESSAGES)),
            pltpu.SemaphoreType.DMA((STEPS, MESSAGES)),
        ],
        compiler_params=pltpu.CompilerParams(
            collective_id=0, has_side_effects=True
        ),
    )(populations, soot_moments, growth_rate, moment_rates)
    anywhere = pl.BlockSpec(memory_space=pl.ANY)
    return pl.pallas_call(
        write_back,
        out_shape=tuple(jax.ShapeDtypeStruct(a.shape, f32) for a in held),
        in_specs=[anywhere] * 2,
        out_specs=(pl.BlockSpec(memory_space=pltpu.HBM),) * 2,
        scratch_shapes=[pltpu.SemaphoreType.DMA((2,))],
        compiler_params=pltpu.CompilerParams(vmem_limit_bytes=1024 * 1024),
    )(*held)


def solution(mesh):
    in_specs = (P(None, "gx", "gy", "gz"), P(None, "gx", "gy", "gz"), P("gx", "gy", "gz"), P())
    out_specs = (P(None, "gx", "gy", "gz"), P(None, "gx", "gy", "gz"))
    return jax.shard_map(shards, mesh=mesh, in_specs=in_specs, out_specs=out_specs, check_vma=False)
```

time: 32.5 us -> 25.1 us (0.77)
  local copies, waits for them, and re-layouts: 5.09 us -> 0 us
  Pallas kernels: 26.5 us -> 24.3 us
    unnamed x10 -> x0, local copies, waits for them, and re-layouts: 5.09 us -> none
    pallas_call x1, Pallas kernels: 26.5 us -> 23.3 us  [shards(): pl.pallas_call(kernel, out_shape=(pltpu.VMEM(populations.shape, f32), plt...]
    pallas_call x0 -> x1, Pallas kernels: none -> 0.99 us  [shards(): pl.pallas_call(write_back, out_shape=tuple((jax.ShapeDtypeStruct(a.shape,...]
where the time goes in v1:
time: 25.1 us; the launch traced here: 25 us
  Pallas kernels  24.3 us (97%)
  between operations  0.64 us (3%)
    pallas_call x1, Pallas kernels, shards(): pl.pallas_call(kernel, out_shape=(pltpu.VMEM(populations.shape, f32), plt...  23.3 us
    pallas_call x1, Pallas kernels, shards(): pl.pallas_call(write_back, out_shape=tuple((jax.ShapeDtypeStruct(a.shape,...  0.99 us

profile of v1, /device:TPU:1, one launch (start us, length us, event | category | flops | bytes accessed | tf_op | source)
XLA Modules:
  0.0 25.0 jit_solution(17050305975186167726)
XLA Ops:
  0.6 23.3 %shard_map.59 = (f32[27,8,8,128]{3,2,1,0:T(8,128)S(1)}, f32[6,8,8,128]{3,2,1,0:T(8,128)S(1)}) custom-call(f32[27,8,8,128]{3,2,1,0:T(8,128)} %pops_ref.1, f32[6,8,8,128]{3,2,1,0:T(8,128)} %soot_ref.1, f32[8,8,128]{2,1,0:T(8,128)} %growth_ref.1, f32[27]{0:T(128)} %rates_ref.1), custom_call_target="tpu_custom_call" | custom-call | tf_op jit(solution)/shard_map/pallas_call | solution.py:373
  24.0 1.0 %shard_map.60 = (f32[27,8,8,128]{3,2,1,0:T(8,128)}, f32[6,8,8,128]{3,2,1,0:T(8,128)}) custom-call(f32[27,8,8,128]{3,2,1,0:T(8,128)S(1)} %get-tuple-element.4.pops_ref, f32[6,8,8,128]{3,2,1,0:T(8,128)S(1)} %get-tuple-element.5.soot_ref), custom_call_target="tpu_custom_call" | custom-call | tf_op jit(solution)/shard_map/pallas_call | solution.py:405

commit v2 on v1

--- a/solution.py
+++ b/solution.py
@@ -189,70 +189,79 @@
             device_id_type=MESH,
         )
 
-    def messages_x(step):
+    def messages_xy(step):
         out = []
         for d, (a, b) in enumerate(CORNERS):
             out.append(message(step, XY + d, xys.at[step, d], xyh.at[step, d], (SPEED[a], SPEED[b], 0)))
+        for d, (a, b) in enumerate(CORNERS):
+            out.append(message(step, XYZ + d, xys.at[step, d], xyzh.at[step, d], (SPEED[a], SPEED[b], 1)))
+        return out
+
+    def messages_x(step):
+        out = []
         for a in SIDES:
             first, slot = (9, 0) if a == 1 else (24, 9)
             there = F.at[step, pl.ds(first, 15), pl.ds(block(slot), 8)]
             out.append(message(step, X + a - 1, xs.at[step, a - 1], there, (SPEED[a], 0, 0)))
-        for d, (a, b) in enumerate(CORNERS):
-            out.append(message(step, XYZ + d, xys.at[step, d], xyzh.at[step, d], (SPEED[a], SPEED[b], 1)))
         for a in SIDES:
             out.append(message(step, XZ + a - 1, xzs.at[step, a - 1], xzh.at[step, a - 1], (SPEED[a], 0, 1)))
         return out
 
-    def messages_yz(step):
+    def messages_y(step):
         out = []
         for b in SIDES:
             out.append(message(step, Y + b - 1, ys.at[step, b - 1], yh.at[step, b - 1], (0, SPEED[b], 0)))
         for b in SIDES:
             out.append(message(step, YZ + b - 1, yzs.at[step, b - 1], yzh.at[step, b - 1], (0, SPEED[b], 1)))
-        out.append(message(step, Z, zs.at[step], zh.at[step], (0, 0, 1)))
         return out
 
-    def packed_of(pairs):
-        total = None
-        for i, (one, two) in enumerate(pairs):
-            value = both(lane, one, two)
-            moved = pltpu.roll(value, 2 * i, 1) if i else value
-            here = (lane == 2 * i) | (lane == (2 * i - 1) % 128)
-            total = moved if total is None else jnp.where(here, moved, total)
-        return total
-
-    def unpacked(total, i):
-        return pltpu.roll(total, 128 - 2 * i, 1) if i else total
-
-    def pack_x(step):
+    def message_z(step):
+        return message(step, Z, zs.at[step], zh.at[step], (0, 0, 1))
+
+    def send_x(step):
         for a in SIDES:
             first, rows = (9, slice(block(8), block(8) + 8)) if a == 1 else (24, slice(block(1), block(1) + 8))
-            values = [F[step, first + i, rows, :] for i in range(15)]
-            for i in range(15):
-                xs[step, a - 1, i] = values[i]
-            xzs[step, a - 1] = packed_of([(values[3 * b + 1], values[3 * b + 2]) for b in range(3)])
+            packed = None
+            for b in range(3):
+                raw = [F[step, pop(a, b, e), rows, :] for e in range(3)]
+                moved = pltpu.roll(jnp.where(lane == 0, raw[2], raw[1]), 2 * b + 1, 1)
+                packed = moved if b == 0 else jnp.where(lane >= 2 * b, moved, packed)
+                for e in range(3):
+                    xs[step, a - 1, 3 * b + e] = turn(raw[e], e)
+            xzs[step, a - 1] = packed
+            for i in range(9, 15):
+                xs[step, a - 1, i] = F[step, first + i, rows, :]
         for d, (a, b) in enumerate(CORNERS):
-            row = block(8 if a == 1 else 1) + (7 if b == 1 else 0)
+            row = 7 if b == 1 else 0
             for e in range(3):
-                xys[step, d, e : e + 1, :] = F[step, pop(a, b, e), row : row + 1, :]
-
-    def pack_y(step):
+                xys[step, d, e : e + 1, :] = xs[step, a - 1, 3 * b + e, row : row + 1, :]
+
+        @pl.when(step == 0)
+        def _():
+            pl.semaphore_wait(barrier, len(targets))
+
+        far, near = messages_xy(step), messages_x(step)
+        for copy in far + near[2:] + near[:2]:
+            copy.start()
+
+    def send_y(step):
         for b in SIDES:
             row = block(1) + (7 if b == 1 else 0)
-            pairs = []
+            packed = None
             for a in range(3):
-                found = [F[step, pop(a, b, e), pl.ds(row, 8, stride=16), :] for e in range(3)]
+                raw = [F[step, pop(a, b, e), pl.ds(row, 8, stride=16), :] for e in range(3)]
+                moved = pltpu.roll(jnp.where(lane == 0, raw[2], raw[1]), 2 * a + 1, 1)
+                packed = moved if a == 0 else jnp.where(lane >= 2 * a, moved, packed)
                 for e in range(3):
-                    ys[step, b - 1, 3 * a + e] = found[e]
-                pairs.append((found[1], found[2]))
-            yzs[step, b - 1] = packed_of(pairs)
+                    ys[step, b - 1, 3 * a + e] = turn(raw[e], e)
+            yzs[step, b - 1] = packed
             for j in range(6):
                 ys[step, b - 1, 9 + j] = F[step, SOOT[1, b] + j, pl.ds(row, 8, stride=16), :]
-
-    def fix_yz(step):
-        for copy in messages_yz(step):
-            copy.wait_recv()
-
+        for copy in messages_y(step):
+            copy.start()
+
+    def fix_z(step):
+        message_z(step).wait_recv()
         plus, minus = zh[step, 0], pltpu.roll(zh[step, 1], 126, 1)
 
         def fix_layers(i, carry):
@@ -266,15 +275,21 @@
             return carry
 
         lax.fori_loop(0, 4, fix_layers, 0)
+
+    def unpacked(packed, i, e):
+        shift = (128 - 2 * i - (0 if e == 1 else 2)) % 128
+        return pltpu.roll(packed, shift, 1) if shift else packed
+
+    def fix_y(step):
+        for copy in messages_y(step):
+            copy.wait_recv()
         for b in SIDES:
             row = block(1) + (-1 if b == 1 else 8)
-            packed = yzh[step, b - 1]
             for a in range(3):
-                moved = unpacked(packed, a)
                 for e in range(3):
                     value = yh[step, b - 1, 3 * a + e]
                     if e:
-                        value = jnp.where(lane == lane_of(e), moved, value)
+                        value = jnp.where(lane == lane_of(e), unpacked(yzh[step, b - 1], a, e), value)
                     F[step, pop(a, b, e), pl.ds(row, 8, stride=16), :] = value
             for j in range(6):
                 F[step, SOOT[1, b] + j, pl.ds(row, 8, stride=16), :] = yh[step, b - 1, 9 + j]
@@ -286,10 +301,12 @@
             slot = 0 if a == 1 else 9
             packed = xzh[step, a - 1]
             for b in range(3):
-                moved = unpacked(packed, b)
                 for e in SIDES:
+                    moved = unpacked(packed, b, e)
                     there = F.at[step, pop(a, b, e), block(slot) : block(slot) + 8, :]
                     pltpu.store(there, moved, mask=lane == lane_of(e))
+        for copy in messages_xy(step):
+            copy.wait_recv()
         other = ((sublane == 1) & (lane == 0)) | ((sublane == 2) & (lane == LAST))
         for d, (a, b) in enumerate(CORNERS):
             row = block(0 if a == 1 else 9) + (-1 if b == 1 else 8)
@@ -304,11 +321,21 @@
     def one_pass(step, carry):
         @pl.when(step > 0)
         def _():
-            fix_yz(step - 1)
-            fix_x(step - 1)
+            fix_z(step - 1)
+            fix_y(step - 1)
+
+        @pl.when(step == STEPS)
+        def _():
+            for copy in messages_y(STEPS - 1) + [message_z(STEPS - 1)]:
+                copy.wait_send()
 
         def two_layers(i, carry):
+            i = lax.rem(i + jnp.where(step == STEPS, 1, 0), 4)
             layers = (jnp.where(i == 0, 0, 2 * i - 1), jnp.where(i == 0, 7, 2 * i))
+
+            @pl.when((step > 0) & (i == 0))
+            def _():
+                fix_x(step - 1)
 
             @pl.when(step > 0)
             def _():
@@ -319,19 +346,10 @@
             def _():
                 for x in layers:
                     layer_out(step, x, pops, soot, R, consts, F, C)
-                for x in layers:
-                    turn_layer(step, x, F, zs)
 
             @pl.when((step < STEPS) & (i == 0))
             def _():
-                pack_x(step)
-
-                @pl.when(step == 0)
-                def _():
-                    pl.semaphore_wait(barrier, len(targets))
-
-                for copy in messages_x(step):
-                    copy.start()
+                send_x(step)
 
             return carry
 
@@ -339,20 +357,26 @@
 
         @pl.when(step < STEPS)
         def _():
-            pack_y(step)
-            for copy in messages_yz(step):
-                copy.start()
+            send_y(step)
+
+            def turn_layers(i, carry):
+                for x in (2 * i, 2 * i + 1):
+                    turn_layer(step, x, F, zs)
+                return carry
+
+            lax.fori_loop(0, 4, turn_layers, 0)
+            message_z(step).start()
+
+        @pl.when((step > 0) & (step < STEPS))
+        def _():
+            for copy in messages_xy(step - 1) + messages_x(step - 1) + messages_y(step - 1) + [message_z(step - 1)]:
+                copy.wait_send()
 
         return carry
 
     lax.fori_loop(0, STEPS + 1, one_pass, 0)
-
-    def finish(step, carry):
-        for copy in messages_x(step) + messages_yz(step):
-            copy.wait_send()
-        return carry
-
-    lax.fori_loop(0, STEPS, finish, 0)
+    for copy in messages_xy(STEPS - 1) + messages_x(STEPS - 1):
+        copy.wait_send()
 
 
 def write_back(pops_ref, soot_ref, pops_out, soot_out, sem):

time: 25.1 us -> 23.9 us (0.952)
  Pallas kernels: 24.3 us -> 23.2 us
    pallas_call x1, Pallas kernels: 23.3 us -> 22.2 us  [shards(): pl.pallas_call(kernel, out_shape=(pltpu.VMEM(populations.shape, f32), plt...]
where the time goes in v2:
time: 23.9 us; the launch traced here: 23.8 us
  Pallas kernels  23.2 us (97%)
  between operations  0.64 us (3%)
    pallas_call x1, Pallas kernels, shards(): pl.pallas_call(kernel, out_shape=(pltpu.VMEM(populations.shape, f32), plt...  22.2 us
    pallas_call x1, Pallas kernels, shards(): pl.pallas_call(write_back, out_shape=tuple((jax.ShapeDtypeStruct(a.shape,...  0.99 us

profile of v2, /device:TPU:1, one launch (start us, length us, event | category | flops | bytes accessed | tf_op | source)
XLA Modules:
  0.0 23.8 jit_solution(10733576208322449965)
XLA Ops:
  0.6 22.2 %shard_map.59 = (f32[27,8,8,128]{3,2,1,0:T(8,128)S(1)}, f32[6,8,8,128]{3,2,1,0:T(8,128)S(1)}) custom-call(f32[27,8,8,128]{3,2,1,0:T(8,128)} %pops_ref.1, f32[6,8,8,128]{3,2,1,0:T(8,128)} %soot_ref.1, f32[8,8,128]{2,1,0:T(8,128)} %growth_ref.1, f32[27]{0:T(128)} %rates_ref.1), custom_call_target="tpu_custom_call" | custom-call | tf_op jit(solution)/shard_map/pallas_call | solution.py:397
  22.8 1.0 %shard_map.60 = (f32[27,8,8,128]{3,2,1,0:T(8,128)}, f32[6,8,8,128]{3,2,1,0:T(8,128)}) custom-call(f32[27,8,8,128]{3,2,1,0:T(8,128)S(1)} %get-tuple-element.4.pops_ref, f32[6,8,8,128]{3,2,1,0:T(8,128)S(1)} %get-tuple-element.5.soot_ref), custom_call_target="tpu_custom_call" | custom-call | tf_op jit(solution)/shard_map/pallas_call | solution.py:429

commit v3 on v2

--- a/solution.py
+++ b/solution.py
@@ -133,9 +133,9 @@
         F[step, two, rows, :] = turn(minus, 2)
         moved = pltpu.roll(jnp.where(lane == 0, minus, plus), 8 * place + 1 + x, 1)
         packed = moved if place == 0 else jnp.where(past >= 8 * place, moved, packed)
-    left = lax.rem(lane, 8)
+    left = lane & 7
     zs[step, 0] = jnp.where(left == x, packed, zs[step, 0])
-    zs[step, 1] = jnp.where(left == lax.rem(x + 1, 8), packed, zs[step, 1])
+    zs[step, 1] = jnp.where(left == ((x + 1) & 7), packed, zs[step, 1])
 
 
 def pull(step, x, F, center, pops, soot_ref):
@@ -159,8 +159,10 @@
     position = tuple(lax.axis_index(axis) for axis in ("gx", "gy", "gz"))
     counts = tuple(lax.axis_size(axis) for axis in ("gx", "gy", "gz"))
 
+    near = [{0: p, 1: lax.rem(p + 1, n), -1: lax.rem(p + (n - 1), n)} for p, n in zip(position, counts)]
+
     def device(*move):
-        return tuple(lax.rem(p + (m + n), n) for p, m, n in zip(position, move, counts))
+        return tuple(at[m] for at, m in zip(near, move))
 
     targets = [(i, j, k) for i in (0, 1, -1) for j in (0, 1, -1) for k in (0, 1) if (i, j, k) != (0, 0, 0)]
     barrier = pltpu.get_barrier_semaphore()
@@ -219,6 +221,19 @@
         return message(step, Z, zs.at[step], zh.at[step], (0, 0, 1))
 
     def send_x(step):
+        for d, (a, b) in enumerate(CORNERS):
+            first = block(8 if a == 1 else 1)
+            row = 7 if b == 1 else 0
+            for e in range(3):
+                value = turn(F[step, pop(a, b, e), first : first + 8, :], e)
+                xys[step, d, e : e + 1, :] = value[row : row + 1, :]
+
+        @pl.when(step == 0)
+        def _():
+            pl.semaphore_wait(barrier, len(targets))
+
+        for copy in messages_xy(step):
+            copy.start()
         for a in SIDES:
             first, rows = (9, slice(block(8), block(8) + 8)) if a == 1 else (24, slice(block(1), block(1) + 8))
             packed = None
@@ -231,17 +246,8 @@
             xzs[step, a - 1] = packed
             for i in range(9, 15):
                 xs[step, a - 1, i] = F[step, first + i, rows, :]
-        for d, (a, b) in enumerate(CORNERS):
-            row = 7 if b == 1 else 0
-            for e in range(3):
-                xys[step, d, e : e + 1, :] = xs[step, a - 1, 3 * b + e, row : row + 1, :]
-
-        @pl.when(step == 0)
-        def _():
-            pl.semaphore_wait(barrier, len(targets))
-
-        far, near = messages_xy(step), messages_x(step)
-        for copy in far + near[2:] + near[:2]:
+        faces = messages_x(step)
+        for copy in faces:
             copy.start()
 
     def send_y(step):
@@ -261,15 +267,15 @@
             copy.start()
 
     def fix_z(step):
-        message_z(step).wait_recv()
+        message_z(step).wait()
         plus, minus = zh[step, 0], pltpu.roll(zh[step, 1], 126, 1)
 
         def fix_layers(i, carry):
             for x in (2 * i, 2 * i + 1):
                 rows = pl.ds(pl.multiple_of(16 * x + 24, 8), 8)
-                packed = jnp.where(lax.rem(lane, 8) == x, plus, minus)
+                packed = jnp.where(lane & 7 == x, plus, minus)
                 for place in range(15):
-                    moved = pltpu.roll(packed, lax.rem(128 - 8 * place - x, 128), 1)
+                    moved = pltpu.roll(packed, (128 - 8 * place - x) & 127, 1)
                     for e, field in zip(SIDES, z_fields(place)):
                         pltpu.store(F.at[step, field, rows, :], moved, mask=lane == lane_of(e))
             return carry
@@ -282,7 +288,7 @@
 
     def fix_y(step):
         for copy in messages_y(step):
-            copy.wait_recv()
+            copy.wait()
         for b in SIDES:
             row = block(1) + (-1 if b == 1 else 8)
             for a in range(3):
@@ -296,7 +302,7 @@
 
     def fix_x(step):
         for copy in messages_x(step):
-            copy.wait_recv()
+            copy.wait()
         for a in SIDES:
             slot = 0 if a == 1 else 9
             packed = xzh[step, a - 1]
@@ -305,14 +311,17 @@
                     moved = unpacked(packed, b, e)
                     there = F.at[step, pop(a, b, e), block(slot) : block(slot) + 8, :]
                     pltpu.store(there, moved, mask=lane == lane_of(e))
-        for copy in messages_xy(step):
-            copy.wait_recv()
+
+    def fix_xy(step):
+        far = messages_xy(step)
+        for copy in far[4:] + far[:4]:
+            copy.wait()
         other = ((sublane == 1) & (lane == 0)) | ((sublane == 2) & (lane == LAST))
         for d, (a, b) in enumerate(CORNERS):
-            row = block(0 if a == 1 else 9) + (-1 if b == 1 else 8)
+            x, row = 0 if a == 1 else 7, 0 if b == 1 else 7
             value = jnp.where(other, xyzh[step, d], xyh[step, d])
             for e in range(3):
-                F[step, pop(a, b, e), row : row + 1, :] = value[e : e + 1, :]
+                pops[9 * a + 3 * b + e, x, row : row + 1, :] = value[e : e + 1, :]
 
     for load in loads:
         load.wait()
@@ -324,11 +333,6 @@
             fix_z(step - 1)
             fix_y(step - 1)
 
-        @pl.when(step == STEPS)
-        def _():
-            for copy in messages_y(STEPS - 1) + [message_z(STEPS - 1)]:
-                copy.wait_send()
-
         def two_layers(i, carry):
             i = lax.rem(i + jnp.where(step == STEPS, 1, 0), 4)
             layers = (jnp.where(i == 0, 0, 2 * i - 1), jnp.where(i == 0, 7, 2 * i))
@@ -342,6 +346,10 @@
                 for x in layers:
                     pull(step - 1, x, F, C, pops, soot)
 
+            @pl.when((step > 0) & (i == 0))
+            def _():
+                fix_xy(step - 1)
+
             @pl.when(step < STEPS)
             def _():
                 for x in layers:
@@ -367,16 +375,9 @@
             lax.fori_loop(0, 4, turn_layers, 0)
             message_z(step).start()
 
-        @pl.when((step > 0) & (step < STEPS))
-        def _():
-            for copy in messages_xy(step - 1) + messages_x(step - 1) + messages_y(step - 1) + [message_z(step - 1)]:
-                copy.wait_send()
-
         return carry
 
     lax.fori_loop(0, STEPS + 1, one_pass, 0)
-    for copy in messages_xy(STEPS - 1) + messages_x(STEPS - 1):
-        copy.wait_send()
 
 
 def write_back(pops_ref, soot_ref, pops_out, soot_out, sem):

time: 23.9 us -> 23.8 us (level)
  no operation moved by 1% of the time
where the time goes in v3:
time: 23.8 us; the launch traced here: 23.7 us
  Pallas kernels  23.1 us (97%)
  between operations  0.64 us (3%)
    pallas_call x1, Pallas kernels, shards(): pl.pallas_call(kernel, out_shape=(pltpu.VMEM(populations.shape, f32), plt...  22.1 us
    pallas_call x1, Pallas kernels, shards(): pl.pallas_call(write_back, out_shape=tuple((jax.ShapeDtypeStruct(a.shape,...  0.99 us

profile of v3, /device:TPU:1, one launch (start us, length us, event | category | flops | bytes accessed | tf_op | source)
XLA Modules:
  0.0 23.7 jit_solution(7900017002255075135)
XLA Ops:
  0.6 22.1 %shard_map.59 = (f32[27,8,8,128]{3,2,1,0:T(8,128)S(1)}, f32[6,8,8,128]{3,2,1,0:T(8,128)S(1)}) custom-call(f32[27,8,8,128]{3,2,1,0:T(8,128)} %pops_ref.1, f32[6,8,8,128]{3,2,1,0:T(8,128)} %soot_ref.1, f32[8,8,128]{2,1,0:T(8,128)} %growth_ref.1, f32[27]{0:T(128)} %rates_ref.1), custom_call_target="tpu_custom_call" | custom-call | tf_op jit(solution)/shard_map/pallas_call | solution.py:398
  22.7 1.0 %shard_map.60 = (f32[27,8,8,128]{3,2,1,0:T(8,128)}, f32[6,8,8,128]{3,2,1,0:T(8,128)}) custom-call(f32[27,8,8,128]{3,2,1,0:T(8,128)S(1)} %get-tuple-element.4.pops_ref, f32[6,8,8,128]{3,2,1,0:T(8,128)S(1)} %get-tuple-element.5.soot_ref), custom_call_target="tpu_custom_call" | custom-call | tf_op jit(solution)/shard_map/pallas_call | solution.py:430

commit v4 on v3

--- a/solution.py
+++ b/solution.py
@@ -106,13 +106,19 @@
     return tuple(SOOT[2, e] + place - 9 for e in SIDES)
 
 
-def layer_out(step, x, pops, soot_ref, growth, consts, F, center):
+def layer_out(step, x, pops, consts, F, U):
     rows = pl.ds(pl.multiple_of(16 * x + 24, 8), 8)
     g = {(k // 9, k // 3 % 3, k % 3): pops[k, x] for k in range(27)}
     n, u = collide(g, consts)
     for (a, b, e), value in n.items():
         F[step, pop(a, b, e), rows, :] = value
-    half = [0.5 * v for v in u]
+    for axis in range(3):
+        U[axis, x] = u[axis]
+
+
+def soot_out(step, x, soot_ref, growth, F, center, U):
+    rows = pl.ds(pl.multiple_of(16 * x + 24, 8), 8)
+    half = [0.5 * U[axis, x] for axis in range(3)]
     for j in range(6):
         soot = soot_ref[j, x]
         for axis in range(3):
@@ -154,7 +160,7 @@
 
 def kernel(
     pops_ref, soot_ref, growth_ref, rates_ref, pops, soot,
-    R, F, C, xs, xzs, xzh, xys, xyh, xyzh, ys, yh, yzs, yzh, zs, zh, rates, consts, load_sem, send_sem, recv_sem,
+    R, F, C, U, xs, xzs, xzh, xys, xyh, xyzh, ys, yh, yzs, yzh, zs, zh, rates, consts, load_sem, send_sem, recv_sem,
 ):
     position = tuple(lax.axis_index(axis) for axis in ("gx", "gy", "gz"))
     counts = tuple(lax.axis_size(axis) for axis in ("gx", "gy", "gz"))
@@ -220,7 +226,7 @@
     def message_z(step):
         return message(step, Z, zs.at[step], zh.at[step], (0, 0, 1))
 
-    def send_x(step):
+    def send_edges(step):
         for d, (a, b) in enumerate(CORNERS):
             first = block(8 if a == 1 else 1)
             row = 7 if b == 1 else 0
@@ -234,6 +240,8 @@
 
         for copy in messages_xy(step):
             copy.start()
+
+    def send_x(step):
         for a in SIDES:
             first, rows = (9, slice(block(8), block(8) + 8)) if a == 1 else (24, slice(block(1), block(1) + 8))
             packed = None
@@ -353,7 +361,16 @@
             @pl.when(step < STEPS)
             def _():
                 for x in layers:
-                    layer_out(step, x, pops, soot, R, consts, F, C)
+                    layer_out(step, x, pops, consts, F, U)
+
+            @pl.when((step < STEPS) & (i == 0))
+            def _():
+                send_edges(step)
+
+            @pl.when(step < STEPS)
+            def _():
+                for x in layers:
+                    soot_out(step, x, soot, R, F, C, U)
 
             @pl.when((step < STEPS) & (i == 0))
             def _():
@@ -404,6 +421,7 @@
             pltpu.VMEM(growth_rate.shape, f32),
             pltpu.VMEM((STEPS, FIELDS, ROWS, 128), f32),
             pltpu.VMEM(soot_moments.shape, f32),
+            pltpu.VMEM((3,) + growth_rate.shape, f32),
             pltpu.VMEM((STEPS, 2, 15, 8, 128), f32),
             pltpu.VMEM((STEPS, 2, 8, 128), f32),
             pltpu.VMEM((STEPS, 2, 8, 128), f32),

time: 23.8 us -> 23.8 us (level)
  no operation moved by 1% of the time
where the time goes in v4:
time: 23.8 us; the launch traced here: 23.7 us
  Pallas kernels  23 us (97%)
  between operations  0.64 us (3%)
    pallas_call x1, Pallas kernels, shards(): pl.pallas_call(kernel, out_shape=(pltpu.VMEM(populations.shape, f32), plt...  22 us
    pallas_call x1, Pallas kernels, shards(): pl.pallas_call(write_back, out_shape=tuple((jax.ShapeDtypeStruct(a.shape,...  0.99 us

profile of v4, /device:TPU:1, one launch (start us, length us, event | category | flops | bytes accessed | tf_op | source)
XLA Modules:
  0.0 23.7 jit_solution(16237941891333072710)
XLA Ops:
  0.6 22.0 %shard_map.59 = (f32[27,8,8,128]{3,2,1,0:T(8,128)S(1)}, f32[6,8,8,128]{3,2,1,0:T(8,128)S(1)}) custom-call(f32[27,8,8,128]{3,2,1,0:T(8,128)} %pops_ref.1, f32[6,8,8,128]{3,2,1,0:T(8,128)} %soot_ref.1, f32[8,8,128]{2,1,0:T(8,128)} %growth_ref.1, f32[27]{0:T(128)} %rates_ref.1), custom_call_target="tpu_custom_call" | custom-call | tf_op jit(solution)/shard_map/pallas_call | solution.py:415
  22.7 1.0 %shard_map.60 = (f32[27,8,8,128]{3,2,1,0:T(8,128)}, f32[6,8,8,128]{3,2,1,0:T(8,128)}) custom-call(f32[27,8,8,128]{3,2,1,0:T(8,128)S(1)} %get-tuple-element.4.pops_ref, f32[6,8,8,128]{3,2,1,0:T(8,128)S(1)} %get-tuple-element.5.soot_ref), custom_call_target="tpu_custom_call" | custom-call | tf_op jit(solution)/shard_map/pallas_call | solution.py:448

commit v5 on v4

--- a/solution.py
+++ b/solution.py
@@ -172,7 +172,7 @@
 
     targets = [(i, j, k) for i in (0, 1, -1) for j in (0, 1, -1) for k in (0, 1) if (i, j, k) != (0, 0, 0)]
     barrier = pltpu.get_barrier_semaphore()
-    for target in sorted(targets, key=lambda t: -abs(t[0])):
+    for target in sorted(targets, key=lambda t: (-abs(t[0]) - abs(t[1]), t[2])):
         pl.semaphore_signal(barrier, inc=1, device_id=device(*target), device_id_type=MESH)
 
     loads = [

time: 23.8 us -> 23.7 us (level)
  no operation moved by 1% of the time
where the time goes in v5:
time: 23.7 us; the launch traced here: 23.6 us
  Pallas kernels  23 us (97%)
  between operations  0.64 us (3%)
    pallas_call x1, Pallas kernels, shards(): pl.pallas_call(kernel, out_shape=(pltpu.VMEM(populations.shape, f32), plt...  22 us
    pallas_call x1, Pallas kernels, shards(): pl.pallas_call(write_back, out_shape=tuple((jax.ShapeDtypeStruct(a.shape,...  0.99 us

profile of v5, /device:TPU:1, one launch (start us, length us, event | category | flops | bytes accessed | tf_op | source)
XLA Modules:
  0.0 23.6 jit_solution(12979212304288451793)
XLA Ops:
  0.6 22.0 %shard_map.59 = (f32[27,8,8,128]{3,2,1,0:T(8,128)S(1)}, f32[6,8,8,128]{3,2,1,0:T(8,128)S(1)}) custom-call(f32[27,8,8,128]{3,2,1,0:T(8,128)} %pops_ref.1, f32[6,8,8,128]{3,2,1,0:T(8,128)} %soot_ref.1, f32[8,8,128]{2,1,0:T(8,128)} %growth_ref.1, f32[27]{0:T(128)} %rates_ref.1), custom_call_target="tpu_custom_call" | custom-call | tf_op jit(solution)/shard_map/pallas_call | solution.py:415
  22.7 1.0 %shard_map.60 = (f32[27,8,8,128]{3,2,1,0:T(8,128)}, f32[6,8,8,128]{3,2,1,0:T(8,128)}) custom-call(f32[27,8,8,128]{3,2,1,0:T(8,128)S(1)} %get-tuple-element.4.pops_ref, f32[6,8,8,128]{3,2,1,0:T(8,128)S(1)} %get-tuple-element.5.soot_ref), custom_call_target="tpu_custom_call" | custom-call | tf_op jit(solution)/shard_map/pallas_call | solution.py:448
